TPU v7x, 32 devices: a whole 2x2x4 slice. The times are simulated.
32 devices in a mesh: grp: 2 (over x), gx: 16 (over z, y, core).
Axes of the slice: x: 2, y: 2, z: 4, core: 2. Of those that a mesh axis runs over, the one named last changes fastest.
Arguments:
- velocity: float32 [6, 256, 64, 128], P('grp', 'gx'), parts along dimension 0, may hold values from -6 to 6
- vfrac_class: int32 [512, 64, 128], P(('grp', 'gx')), parts along dimension 0, may hold values from 0 to 3
- cut_cells: int32 [32768], P(('grp', 'gx')), parts along dimension 0, may hold values from 1 to 131070, as said below
- cut_count: int32 [32], P(('grp', 'gx')), parts along dimension 0, may hold values from 128 to 1024, as said below
- offsets: int32 [18, 16384], P('grp', 'gx'), parts along dimension 0, may hold values from 0 to 26, as said below
Outputs:
- projected: float32 [6, 256, 64, 128], P('grp', 'gx'), parts along dimension 0
- potential: float32 [512, 64, 128], P(('grp', 'gx')), parts along dimension 0
There are 2 independent parts, one for each index of `grp`. A program takes and returns all parts, laid end to end along the dimension named above; each array names one. Nothing has to cross between parts.
Inputs may be any that keep to these rules, and one draw needn't show every extreme that they name: `cut_cells`: each device's block of 1024 entries holds distinct local cell numbers x * 64 * 128 + y * 128 + z of that device's cells, with z from 1 to 126; in every group of four slots the first cell has x = 0, the second x = 15, the other two x from 1 to 14. `cut_count`: some devices have all 1024 slots live, most have fewer. `offsets`: code (dx + 1) * 9 + (dy + 1) * 3 + (dz + 1) of a cell of the 3 x 3 x 3 block around the cut cell; entry 0 is 13, the cut cell itself; entries 1 and 2 have dx = -1, entries 3 and 4 have dx = 1, the others dx = 0; the 9 codes of one slot are distinct.
All inputs are finite; a program needn't handle non-finite values. Where the computation divides by a largest or mean magnitude, that divisor is 1e-20 or more.
Results may differ from a plain program's by a relative error of at most 0.0003.
Values sent between devices are 32-bit elements; how exact they have to be, the bound alone decides.
A program may use at most 320 MiB of HBM per device.

v0:
```python
import jax
import jax.numpy as jnp
from jax import lax
from jax.sharding import PartitionSpec as P

LEVELS = 3
CYCLES = 2
SWEEPS = 2
COARSE = 4


courant = 0.5
damping = 0.8


def with_halo(block, sides, width):
    for axis, dim in sides:
        count = lax.axis_size(axis)
        forward = [(i, i + 1) for i in range(count - 1)]
        forward.append((count - 1, 0))
        backward = [(target, source) for source, target in forward]
        low = lax.ppermute(
            lax.slice_in_dim(block, block.shape[dim] - width, None, axis=dim), axis, forward
        )
        high = lax.ppermute(lax.slice_in_dim(block, 0, width, axis=dim), axis, backward)
        block = jnp.concatenate([low, block, high], axis=dim)
    return block


def shifted(value, axis, steps):
    count = lax.axis_size(axis)
    pairs = [(source, (source + steps) % count) for source in range(count)]
    return lax.ppermute(value, axis, pairs)


def minmod_limit(first_diff, second_diff):
    return (
        0.5
        * (jnp.sign(first_diff) + jnp.sign(second_diff))
        * jnp.minimum(jnp.abs(first_diff), jnp.abs(second_diff))
    )


def take_span(array, begin, finish, direction):
    return lax.slice_in_dim(array, begin, finish, axis=direction)


def face_balance(state_pad, speed_pad, fraction_pad, direction, walled):
    cell_count = state_pad.shape[direction] - 4
    middle = take_span(state_pad, 1, cell_count + 3, direction)
    slopes = minmod_limit(
        middle - take_span(state_pad, 0, cell_count + 2, direction),
        take_span(state_pad, 2, cell_count + 4, direction) - middle,
    )
    left_side = take_span(middle + 0.5 * slopes, 0, cell_count + 1, direction)
    right_side = take_span(middle - 0.5 * slopes, 1, cell_count + 2, direction)
    speed_mid = take_span(speed_pad, 1, cell_count + 3, direction)
    fraction_mid = take_span(fraction_pad, 1, cell_count + 3, direction)
    face_speed = 0.5 * (
        take_span(speed_mid, 0, cell_count + 1, direction)
        + take_span(speed_mid, 1, cell_count + 2, direction)
    )
    aperture = jnp.minimum(
        take_span(fraction_mid, 0, cell_count + 1, direction),
        take_span(fraction_mid, 1, cell_count + 2, direction),
    )
    fluxes = aperture * face_speed * jnp.where(face_speed > 0, left_side, right_side)
    if walled:
        edge_zero = jnp.zeros_like(take_span(fluxes, 0, 1, direction))
        fluxes = jnp.concatenate(
            [edge_zero, take_span(fluxes, 1, cell_count, direction), edge_zero], axis=direction
        )
    return take_span(fluxes, 1, cell_count + 1, direction) - take_span(
        fluxes, 0, cell_count, direction
    )


def advect_balance(velocity, fraction, velocity_xpad, fraction_xpad):
    along_x = face_balance(velocity_xpad, velocity_xpad[0:1], fraction_xpad, 1, False)
    y_state = jnp.pad(velocity, ((0, 0), (0, 0), (2, 2), (0, 0)), mode="wrap")
    y_fraction = jnp.pad(fraction[None], ((0, 0), (0, 0), (2, 2), (0, 0)), mode="wrap")
    along_y = face_balance(y_state, y_state[1:2], y_fraction, 2, False)
    z_state = jnp.pad(velocity, ((0, 0), (0, 0), (0, 0), (2, 2)), mode="edge")
    z_fraction = jnp.pad(fraction[None], ((0, 0), (0, 0), (0, 0), (2, 2)), mode="edge")
    along_z = face_balance(z_state, z_state[2:3], z_fraction, 3, True)
    return along_x + along_y + along_z


def divergence(x_padded, advanced):
    along_x = x_padded[2:] - x_padded[:-2]
    along_y = jnp.roll(advanced[1], -1, axis=1) - jnp.roll(advanced[1], 1, axis=1)
    z_padded = jnp.pad(advanced[2], ((0, 0), (0, 0), (1, 1)))
    along_z = z_padded[:, :, 2:] - z_padded[:, :, :-2]
    return 0.5 * (along_x + along_y + along_z)


def gradient(x_padded, estimate):
    along_x = 0.5 * (x_padded[2:] - x_padded[:-2])
    along_y = 0.5 * (jnp.roll(estimate, -1, axis=1) - jnp.roll(estimate, 1, axis=1))
    z_padded = jnp.pad(estimate, ((0, 0), (0, 0), (1, 1)), mode="edge")
    along_z = 0.5 * (z_padded[:, :, 2:] - z_padded[:, :, :-2])
    return jnp.stack([along_x, along_y, along_z])


def neighbour_sum(padded):
    middle = padded[1:-1]
    z_padded = jnp.pad(middle, ((0, 0), (0, 0), (1, 1)), mode="edge")
    return (
        padded[2:]
        + padded[:-2]
        + (jnp.roll(middle, -1, axis=1) + jnp.roll(middle, 1, axis=1))
        + (z_padded[:, :, 2:] + z_padded[:, :, :-2])
    )


def relax(middle, neighbours, source, spacing_sq):
    return middle + damping / 6.0 * (neighbours - 6.0 * middle - spacing_sq * source)


def restrict_field(values):
    x_size, y_size, z_size = values.shape
    return jnp.mean(values.reshape(x_size // 2, 2, y_size // 2, 2, z_size // 2, 2), axis=(1, 3, 5))


def prolong_field(values):
    return jnp.repeat(jnp.repeat(jnp.repeat(values, 2, axis=0), 2, axis=1), 2, axis=2)


def single_rim(values):
    return with_halo(values, (("gx", 0),), 1)


def smooth_level(estimate, source, spacing_sq, turns):
    for sweep_index in range(turns):
        estimate = relax(estimate, neighbour_sum(single_rim(estimate)), source, spacing_sq)
    return estimate


def vcycle(estimate, source, depth_level):
    spacing_sq = float(4**depth_level)
    if depth_level == LEVELS - 1:
        return smooth_level(estimate, source, spacing_sq, COARSE)
    estimate = smooth_level(estimate, source, spacing_sq, SWEEPS)
    residue = source - (neighbour_sum(single_rim(estimate)) - 6.0 * estimate) / spacing_sq
    coarse_source = restrict_field(residue)
    correction = vcycle(jnp.zeros_like(coarse_source), coarse_source, depth_level + 1)
    estimate = estimate + prolong_field(correction)
    return smooth_level(estimate, source, spacing_sq, SWEEPS)


def local(velocity, vfrac_class, cut_cells, cut_count, offsets):
    x_cells, y_cells, z_cells = vfrac_class.shape
    cell_total = x_cells * y_cells * z_cells
    fraction = 0.25 * vfrac_class.astype(jnp.float32) + 0.25
    velocity_xpad, fraction_xpad = (
        with_halo(velocity, (("gx", 1),), 2),
        with_halo(fraction[None], (("gx", 1),), 2),
    )
    peak_speed = lax.pmax(jnp.max(jnp.abs(velocity)), "gx")
    timestep = courant / (peak_speed + 1e-06)
    balance = advect_balance(velocity, fraction, velocity_xpad, fraction_xpad)
    live_count = cut_count[0]
    active = (jnp.arange(cut_cells.shape[0], dtype=jnp.int32) < live_count).astype(jnp.float32)
    x_local = cut_cells // (y_cells * z_cells)
    y_index = cut_cells // z_cells % y_cells
    z_index = cut_cells % z_cells
    x_target = x_local[None] + offsets // 9 - 1
    y_target = (y_index[None] + offsets // 3 % 3 - 1) % y_cells
    z_target = z_index[None] + offsets % 3 - 1
    hood_sum = jnp.sum(fraction_xpad[0, x_target + 2, y_target, z_target], axis=0)
    cut_balance = balance.reshape(3, cell_total)[:, cut_cells]
    amount = -timestep * cut_balance / hood_sum * active
    spread = jnp.broadcast_to(amount[:, None, :], (3,) + offsets.shape).reshape(3, -1)
    place = (((x_target + 1) * y_cells + y_target) * z_cells + z_target).reshape(-1)
    widened = (
        jnp.zeros((3, (x_cells + 2) * y_cells * z_cells), jnp.float32).at[:, place].add(spread)
    )
    widened = widened.reshape(3, x_cells + 2, y_cells, z_cells)
    from_next = shifted(widened[:, 0], "gx", -1)
    from_prior = shifted(widened[:, -1], "gx", 1)
    moved = widened[:, 1:-1].at[:, -1].add(from_next).at[:, 0].add(from_prior)
    cut_mask = (
        jnp.zeros((cell_total,), jnp.float32).at[cut_cells].add(active).reshape(fraction.shape)
    )
    update = -balance / fraction
    advanced = velocity + timestep * update * (1.0 - cut_mask) + moved
    x_velocity_pad = with_halo(advanced[0], (("gx", 0),), 1)
    source = divergence(x_velocity_pad, advanced)
    potential = jnp.zeros_like(source)
    for cycle_index in range(CYCLES):
        potential = vcycle(potential, source, 0)
    potential_pad = with_halo(potential, (("gx", 0),), 1)
    projected = advanced - gradient(potential_pad, potential)
    return (projected, potential)


def solution(mesh):
    placed = (
        P("grp", "gx", None, None),
        P(("grp", "gx"), None, None),
        P(("grp", "gx")),
        P(("grp", "gx")),
        P("grp", "gx"),
    )
    return jax.shard_map(
        local,
        mesh=mesh,
        in_specs=placed,
        out_specs=(P("grp", "gx", None, None), P(("grp", "gx"), None, None)),
        check_vma=False,
    )
```

profile of v0, /device:TPU:0, one launch (start us, length us, event | category | flops | bytes accessed | tf_op | source)
XLA Modules:
  0.0 780.3 jit_solution(14163331657105433390)
XLA Ops:
  1.7 5.0 collective-permute-start.6
  6.7 1.8 fusion.274
  8.5 2.0 multiply_add_fusion
  11.2 4.4 collective-permute-start.1
  15.6 3.4 pad_maximum_fusion.6
  20.7 2.2 fusion.273
  22.9 1.9 copy.108
  24.9 1.9 copy.107
  27.8 5.1 pad_maximum_fusion.2
  38.2 9.0 %sort = (s32[9216]{0:T(1024)}, s32[9216]{0:T(1024)S(1)}) sort(s32[9216]{0:T(1024)} %bitcast.93, s32[9216]{0:T(1024)S(1)} %iota.6), dimensions={0}, to_apply=%compare | sort | flops 129024 | bytes 147456 | tf_op jit(solution)/shard_map/scatter-add | solution.py:176
  47.8 6.4 scatter_custom_fusion
  57.4 11.0 %fusion.271 = (f32[3,16,64,129]{3,2,1,0:T(8,128)}, f32[3,16,64,129]{3,2,1,0:T(8,128)}, f32[3,16,64,129]{3,2,1,0:T(8,128)}, f32[3,16,64,129]{3,2,1,0:T(8,128)}) fusion(f32[3,16,64,130]{3,2,1,0:T(8,128)} %get-tuple-element.45, f32[3,16,64,130]{3,2,1,0:T(8,128)} %get-tuple-element.46), kind=kLoop, calls=%fused_computation.501 | loop fusion | bytes 12681216 | tf_op jit(solution)/shard_map/slice | solution.py:45
  69.3 4.1 fusion.11
  74.8 4.3 fusion.15
  79.7 4.4 collective-permute-start.3
  85.7 74.0 %gather_fusion.1 = f32[9216]{0:T(1024)S(1)} fusion(f32[1,20,64,128]{3,2,1,0:T(8,128)S(1)} %pad_maximum_fusion.12, s32[9216]{0:T(1024)S(1)} %reshape.328), kind=kCustom, calls=%fused_computation.1 | custom fusion | bytes 221184 | tf_op jit(solution)/shard_map/gather | solution.py:170
  164.4 1.8 fusion.17
  166.3 33.6 %copy.85 = f32[3,16,64,128]{0,3,2,1:T(8,128)} copy(f32[3,16,64,128]{3,2,1,0:T(8,128)} %fusion.17) | data formatting | bytes 3145728 | tf_op jit(solution)/shard_map/add | solution.py:86
  199.9 10.5 %gather_fusion = f32[1024,3]{1,0:T(8,128)S(1)} fusion(f32[3,131072]{0,1:T(8,128)} %bitcast.12, s32[1024]{0:T(1024)S(1)} %copy-done.19), kind=kCustom, calls=%fused_computation | custom fusion | bytes 28672 | tf_op jit(solution)/shard_map/gather | solution.py:171
  210.6 35.0 %pmax.7 = f32[]{:T(128)} all-reduce(f32[]{:T(128)} %get-tuple-element.58), channel_id=1, replica_groups=mesh['grp'=2,'gx'=16] {'gx'}, use_global_device_ids=true, to_apply=%region_1.0 | all-reduce | flops 1 | bytes 8 | tf_op jit(solution)/shard_map/pmax | solution.py:159
  246.6 2.6 broadcast_in_dim.133
  249.3 135.1 %scatter_custom_fusion.1 = f32[3,147456]{0,1:T(8,128)} fusion(s32[9216]{0:T(1024)} %get-tuple-element.26, f32[]{:T(128)} %constant.216.clone.1, f32[9216,3]{1,0:T(8,128)} %bitcast.78, s32[9216]{0:T(1024)} %broadcast_clamp_fusion), kind=kCustom, calls=%fused_computation.5 | custom fusion | flops 27648 | bytes 1769984 | tf_op jit(solution)/shard_map/scatter-add | solution.py:176
  384.4 9.8 %fusion.270 = (f32[3,1,64,128]{0,3,2,1:T(8,128)}, f32[3,1,64,128]{0,3,2,1:T(8,128)}, f32[3,1,64,128]{0,3,2,1:T(8,128)}) fusion(f32[3,18,64,128]{0,3,2,1:T(8,128)} %bitcast.16), kind=kLoop, calls=%fused_computation.500 | loop fusion | bytes 589824 | tf_op jit(solution)/shard_map/slice | solution.py:180
  394.2 2.8 copy.111
  397.2 44.1 %slice.1774 = f32[3,16,64,128]{0,3,2,1:T(8,128)} slice(f32[3,18,64,128]{0,3,2,1:T(8,128)} %bitcast.16), slice={[0:3], [1:17], [0:64], [0:128]} | slice | bytes 3145728 | tf_op jit(solution)/shard_map/slice | solution.py:181
  441.3 39.2 %copy.109 = f32[3,16,64,128]{3,2,1,0:T(8,128)} copy(f32[3,16,64,128]{0,3,2,1:T(8,128)} %slice.1774) | data formatting | bytes 3145728
  480.5 2.8 copy.110
  483.3 2.9 copy.112
  487.5 5.6 collective-permute-done.5
  494.6 2.5 add_add_fusion
  498.2 4.4 collective-permute-start.8
  505.8 4.5 collective-permute-start.10
  513.6 4.5 collective-permute-start.14
  520.3 34.9 %reshape.304 = f32[8,2,32,2,64,2]{5,4,3,2,1,0:T(8,128)} reshape(f32[16,64,128]{2,1,0:T(8,128)S(1)} %fusion.106) | data formatting | bytes 1048576 | tf_op jit(solution)/shard_map/reshape | solution.py:122
  555.2 12.2 %reduce_sum.46 = f32[8,32,64]{2,1,0:T(8,128)S(1)} reduce(f32[8,2,32,2,64,2]{5,4,3,2,1,0:T(8,128)} %reshape.304, f32[]{:T(128)} %constant.216.clone.1), dimensions={1,3,5}, to_apply=%region_5.6 | reduce | flops 114688 | bytes 589828 | tf_op jit(solution)/shard_map/reduce_sum | solution.py:122
  568.9 4.0 collective-permute-start.16
  574.7 4.5 collective-permute-start.20
  580.8 5.7 reshape.305
  586.6 2.6 reduce_sum.47
  589.4 4.5 collective-permute-start.22
  595.5 4.5 collective-permute-start.24
  601.6 4.5 collective-permute-start.26
  608.1 4.5 collective-permute-start.28
  614.4 4.5 collective-permute-start.30
  622.1 4.5 collective-permute-start.32
  629.1 4.4 collective-permute-start.34
  633.5 1.7 collective-permute-done.35
  636.1 4.5 collective-permute-start.36
  643.1 4.7 collective-permute-start.38
  650.3 4.5 collective-permute-start.40
  656.9 34.9 %reshape.312 = f32[8,2,32,2,64,2]{5,4,3,2,1,0:T(8,128)} reshape(f32[16,64,128]{2,1,0:T(8,128)S(1)} %fusion.68) | data formatting | bytes 1048576 | tf_op jit(solution)/shard_map/reshape | solution.py:122
  691.8 12.2 %reduce_sum.48 = f32[8,32,64]{2,1,0:T(8,128)S(1)} reduce(f32[8,2,32,2,64,2]{5,4,3,2,1,0:T(8,128)} %reshape.312, f32[]{:T(128)} %constant.216.clone.1), dimensions={1,3,5}, to_apply=%region_7.8 | reduce | flops 114688 | bytes 589828 | tf_op jit(solution)/shard_map/reduce_sum | solution.py:122
  704.3 4.5 collective-permute-start.42
  710.6 4.5 collective-permute-start.44
  716.7 5.7 reshape.313
  722.4 2.6 reduce_sum.49
  725.1 4.5 collective-permute-start.46
  731.2 4.5 collective-permute-start.48
  737.3 4.5 collective-permute-start.50
  743.9 4.5 collective-permute-start.52
  750.2 4.5 collective-permute-start.54
  757.8 4.5 collective-permute-start.56
  764.9 4.4 collective-permute-start.58
  771.9 4.4 collective-permute-start.60
  (362 shorter events, 83.0 us)
Async XLA Ops:
  1.2 501.5 %collective-permute-start.7 = (f32[1,64,128]{2,1,0:T(8,128)}, f32[1,64,128]{2,1,0:T(8,128)}, u32[]{:S(2)}, u32[]{:S(2)}) collective-permute-start(f32[1,64,128]{2,1,0:T(8,128)} %broadcast.316), channel_id=1, source_target_pairs={{0,1},{1,2},{2,3},{3,4},{4,5},{5,6},{6,7},{7,8},{8,9},{9,10},{10,1... | collective-permute-start | bytes 98312 | tf_op jit(solution)/shard_map/ppermute | solution.py:22
  1.7 501.1 %collective-permute-start.6 = (f32[1,64,128]{2,1,0:T(8,128)}, f32[1,64,128]{2,1,0:T(8,128)}, u32[]{:S(2)}, u32[]{:S(2)}) collective-permute-start(f32[1,64,128]{2,1,0:T(8,128)} %broadcast.316), channel_id=1, source_target_pairs={{1,0},{2,1},{3,2},{4,3},{5,4},{6,5},{7,6},{8,7},{9,8},{10,9},{11,1... | collective-permute-start | bytes 98312 | tf_op jit(solution)/shard_map/ppermute | solution.py:25
  8.5 151.2 %collective-permute-start.2 = (f32[3,2,64,128]{3,2,1,0:T(8,128)}, f32[3,2,64,128]{3,2,1,0:T(8,128)S(1)}, u32[]{:S(2)}, u32[]{:S(2)}) collective-permute-start(f32[3,2,64,128]{3,2,1,0:T(8,128)} %get-tuple-element.63), channel_id=1, source_target_pairs={{0,1},{1,2},{2,3},{3,4},{4,5},{5,6},{6,7},{7,8},{8,9},{9,10},{10,1... | collective-permute-start | bytes 589832 | tf_op jit(solution)/shard_map/ppermute | solution.py:22
  11.2 68.6 %collective-permute-start.1 = (f32[1,2,64,128]{3,2,1,0:T(8,128)}, f32[1,2,64,128]{3,2,1,0:T(8,128)S(1)}, u32[]{:S(2)}, u32[]{:S(2)}) collective-permute-start(f32[1,2,64,128]{3,2,1,0:T(8,128)} %get-tuple-element.156), channel_id=1, source_target_pairs={{1,0},{2,1},{3,2},{4,3},{5,4},{6,5},{7,6},{8,7},{9,8},{10,9},{11,1... | collective-permute-start | bytes 196616 | tf_op jit(solution)/shard_map/ppermute | solution.py:25
  15.6 68.6 %collective-permute-start = (f32[1,2,64,128]{3,2,1,0:T(8,128)}, f32[1,2,64,128]{3,2,1,0:T(8,128)S(1)}, u32[]{:S(2)}, u32[]{:S(2)}) collective-permute-start(f32[1,2,64,128]{3,2,1,0:T(8,128)} %get-tuple-element.155), channel_id=1, source_target_pairs={{0,1},{1,2},{2,3},{3,4},{4,5},{5,6},{6,7},{7,8},{8,9},{9,10},{10,1... | collective-permute-start | bytes 196616 | tf_op jit(solution)/shard_map/ppermute | solution.py:22
  79.7 81.2 %collective-permute-start.3 = (f32[3,2,64,128]{3,2,1,0:T(8,128)}, f32[3,2,64,128]{3,2,1,0:T(8,128)S(1)}, u32[]{:S(2)}, u32[]{:S(2)}) collective-permute-start(f32[3,2,64,128]{3,2,1,0:T(8,128)} %get-tuple-element.64), channel_id=1, source_target_pairs={{1,0},{2,1},{3,2},{4,3},{5,4},{6,5},{7,6},{8,7},{9,8},{10,9},{11,1... | collective-permute-start | bytes 589832 | tf_op jit(solution)/shard_map/ppermute | solution.py:25
  84.8 482.6 %collective-permute-start.13 = (f32[1,32,64]{2,1,0:T(8,128)}, f32[1,32,64]{2,1,0:T(8,128)}, u32[]{:S(2)}, u32[]{:S(2)}) collective-permute-start(f32[1,32,64]{2,1,0:T(8,128)} %broadcast.319), channel_id=1, source_target_pairs={{0,1},{1,2},{2,3},{3,4},{4,5},{5,6},{6,7},{7,8},{8,9},{9,10},{10,1... | collective-permute-start | bytes 24584 | tf_op jit(solution)/shard_map/ppermute | solution.py:22
  166.3 33.6 %copy-start.19 = (s32[1024]{0:T(1024)S(1)}, s32[1024]{0:T(1024)}, u32[]{:S(2)}) copy-start(s32[1024]{0:T(1024)} %get-tuple-element.274) | copy-start | bytes 12292
  166.3 80.1 %copy-start.21 = (f32[1024]{0:T(1024)S(1)}, f32[1024]{0:T(1024)}, u32[]{:S(2)}) copy-start(f32[1024]{0:T(1024)} %copy-done.20) | copy-start | bytes 12292
  397.0 89.8 %collective-permute-start.4 = (f32[3,64,128]{2,1,0:T(8,128)S(1)}, f32[3,64,128]{2,1,0:T(8,128)S(1)}, u32[]{:S(2)}, u32[]{:S(2)}) collective-permute-start(f32[3,64,128]{2,1,0:T(8,128)S(1)} %bitcast.94), channel_id=1, source_target_pairs={{0,15},{1,0},{2,1},{3,2},{4,3},{5,4},{6,5},{7,6},{8,7},{9,8},{10,9... | collective-permute-start | bytes 294920 | tf_op jit(solution)/shard_map/ppermute | solution.py:33
  486.3 6.8 collective-permute-start.5
  498.2 6.0 collective-permute-start.9
  498.2 6.0 collective-permute-start.8
  502.7 64.7 %collective-permute-start.12 = (f32[1,32,64]{2,1,0:T(8,128)}, f32[1,32,64]{2,1,0:T(8,128)S(1)}, u32[]{:S(2)}, u32[]{:S(2)}) collective-permute-start(f32[1,32,64]{2,1,0:T(8,128)} %broadcast.319), channel_id=1, source_target_pairs={{1,0},{2,1},{3,2},{4,3},{5,4},{6,5},{7,6},{8,7},{9,8},{10,9},{11,1... | collective-permute-start | bytes 24584 | tf_op jit(solution)/shard_map/ppermute | solution.py:25
  502.8 86.3 %collective-permute-start.19 = (f32[1,16,32]{2,1,0:T(8,128)S(1)}, f32[1,16,32]{2,1,0:T(8,128)S(1)}, u32[]{:S(2)}, u32[]{:S(2)}) collective-permute-start(f32[1,16,32]{2,1,0:T(8,128)S(1)} %broadcast.323), channel_id=1, source_target_pairs={{0,1},{1,2},{2,3},{3,4},{4,5},{5,6},{6,7},{7,8},{8,9},{9,10},{10,1... | collective-permute-start | bytes 6152 | tf_op jit(solution)/shard_map/ppermute | solution.py:22
  505.7 6.1 collective-permute-start.11
  505.8 6.1 collective-permute-start.10
  513.5 6.1 collective-permute-start.15
  513.6 6.2 collective-permute-start.14
  519.6 69.6 %collective-permute-start.18 = (f32[1,16,32]{2,1,0:T(8,128)S(1)}, f32[1,16,32]{2,1,0:T(8,128)S(1)}, u32[]{:S(2)}, u32[]{:S(2)}) collective-permute-start(f32[1,16,32]{2,1,0:T(8,128)S(1)} %broadcast.323), channel_id=1, source_target_pairs={{1,0},{2,1},{3,2},{4,3},{5,4},{6,5},{7,6},{8,7},{9,8},{10,9},{11,1... | collective-permute-start | bytes 6152 | tf_op jit(solution)/shard_map/ppermute | solution.py:25
  568.4 5.9 collective-permute-start.17
  568.9 5.4 collective-permute-start.16
  574.7 5.9 collective-permute-start.21
  574.7 5.9 collective-permute-start.20
  589.3 5.8 collective-permute-start.23
  589.4 5.8 collective-permute-start.22
  595.4 5.8 collective-permute-start.25
  595.5 5.8 collective-permute-start.24
  601.5 5.8 collective-permute-start.27
  601.6 5.8 collective-permute-start.26
  608.0 5.9 collective-permute-start.29
  608.1 5.9 collective-permute-start.28
  614.3 5.9 collective-permute-start.31
  614.4 5.9 collective-permute-start.30
  622.0 6.2 collective-permute-start.33
  622.1 6.1 collective-permute-start.32
  629.0 6.2 collective-permute-start.35
  629.1 6.1 collective-permute-start.34
  636.1 6.1 collective-permute-start.37
  636.1 6.1 collective-permute-start.36
  643.0 6.1 collective-permute-start.39
  643.1 6.3 collective-permute-start.38
  650.3 6.1 collective-permute-start.41
  650.3 6.1 collective-permute-start.40
  704.2 5.9 collective-permute-start.43
  704.3 5.9 collective-permute-start.42
  710.5 5.9 collective-permute-start.45
  710.6 5.9 collective-permute-start.44
  725.1 5.8 collective-permute-start.47
  725.1 5.8 collective-permute-start.46
  731.2 5.8 collective-permute-start.49
  731.2 5.8 collective-permute-start.48
  737.3 5.8 collective-permute-start.51
  737.3 5.8 collective-permute-start.50
  743.8 5.9 collective-permute-start.53
  743.9 5.9 collective-permute-start.52
  750.1 5.9 collective-permute-start.55
  750.2 5.9 collective-permute-start.54
  757.8 6.2 collective-permute-start.57
  757.8 6.1 collective-permute-start.56
  764.8 6.2 collective-permute-start.59
  764.9 6.1 collective-permute-start.58
  771.8 6.1 collective-permute-start.61
  771.9 6.0 collective-permute-start.60
  (26 other events, 179.4 us)
where the time goes:
time: 787 us; the launch traced here: 780 us
  local copies, waits for them, and re-layouts  344 us (44%)
  other arithmetic  226 us (29%)
  starting transfers between devices  129 us (16%)
  waiting for transfers between devices  42.3 us (5%)
  blocking collectives  35 us (4%)
    scatter-add x3, other arithmetic, local(): jnp.zeros((3, (x_cells + 2) * y_cells * z_cells), jnp.float32).at[:, place]  145 us
    ppermute x30, starting transfers between devices, with_halo(): lax.ppermute(lax.slice_in_dim(block, 0, width, axis=dim), axis, backward)  126 us
    reshape x4, local copies, waits for them, and re-layouts, restrict_field(): values.reshape(x_size // 2, 2, y_size // 2, 2, z_size // 2, 2)  81.2 us
    gather x2, local copies, waits for them, and re-layouts, local(): fraction_xpad[0, x_target + 2, y_target, z_target]  74 us
    unnamed x64, local copies, waits for them, and re-layouts  56.2 us
    slice x1, local copies, waits for them, and re-layouts, local(): moved = widened[:, 1:-1].at[:, -1].add(from_next).at[:, 0].add(from_prior)  44.1 us
    ppermute x30, waiting for transfers between devices, with_halo(): lax.ppermute(lax.slice_in_dim(block, block.shape[dim] - width, None, axis...  35.3 us
    pmax x1, blocking collectives, local(): peak_speed = lax.pmax(jnp.max(jnp.abs(velocity)), 'gx')  35 us
  transfers between devices with their start and end apart: 62, of which 42 were waited for; matrix products, arithmetic and copies ran while one was open for 64% of the time, Pallas kernels for 0%

commit v1 on v0

v1 whole, which is shorter than its diff:
```python
import functools

import jax
import jax.numpy as jnp
from jax import lax
from jax.experimental import pallas as pl
from jax.experimental.pallas import tpu as pltpu
from jax.sharding import PartitionSpec as P

MESH = pl.DeviceIdType.MESH
CYCLES = 2
COURANT = 0.5
DAMP = 0.8
WEIGHT = DAMP / 6.0
VH = 3
FH = 2
PAD = 5
SH = 4


def roll(value, shift, axis):
    size = value.shape[axis]
    return pltpu.roll(value, shift % size, axis)


def lanes(shape):
    return lax.broadcasted_iota(jnp.int32, shape, len(shape) - 1)


def minmod(a, b):
    return jnp.maximum(jnp.minimum(a, b), 0.0) + jnp.minimum(jnp.maximum(a, b), 0.0)


def kernel(
    n, vel_hbm, vf_hbm, lists_hbm, proj_ref, pot_ref,
    vp, vfp, lists, mx, frr, mask_ref, bal, amt, moved, rolled, fx, sx, spread_t,
    u_halo, f0, p0a, p0b, land0, f1, p1a, p1b, land1, f2, p2a, p2b, land2, tmp, tmp1,
    bar_send, bar_recv, load_sem, send_sem, recv_sem,
):
    me = lax.axis_index("gx")
    right, left = lax.rem(me + 1, n), lax.rem(me + n - 1, n)
    cx, ny, nz = pot_ref.shape
    shift_z = nz.bit_length() - 1
    slots = lists.shape[2]

    loads = [
        pltpu.make_async_copy(vel_hbm, vp.at[:, VH : VH + cx], load_sem.at[0]),
        pltpu.make_async_copy(vf_hbm, vfp.at[FH : FH + cx], load_sem.at[1]),
        pltpu.make_async_copy(lists_hbm, lists.at[0], load_sem.at[2]),
    ]
    for load in loads:
        load.start()

    barrier = pltpu.get_barrier_semaphore()

    def greet(d, carry):
        pl.semaphore_signal(
            barrier, inc=1, device_id={"gx": lax.rem(me + d, n)}, device_id_type=MESH
        )
        return carry

    lax.fori_loop(1, n, greet, 0)
    pl.semaphore_wait(barrier, n - 1)

    used = [0]

    def send(src, dst, target):
        index = used[0]
        used[0] += 1
        copy = pltpu.make_async_remote_copy(
            src_ref=src, dst_ref=dst, send_sem=send_sem.at[index], recv_sem=recv_sem.at[index],
            device_id={"gx": target}, device_id_type=MESH,
        )
        copy.start()
        return copy

    first = [
        send(vel_hbm.at[:, cx - VH : cx], vp.at[:, 0:VH], right),
        send(vel_hbm.at[:, 0:VH], vp.at[:, VH + cx : VH + cx + VH], left),
        send(vf_hbm.at[cx - FH : cx], vfp.at[0:FH], right),
        send(vf_hbm.at[0:FH], vfp.at[FH + cx : FH + cx + FH], left),
        send(lists_hbm, lists.at[1], right),
        send(lists_hbm, lists.at[2], left),
    ]

    loads[0].wait()

    def peak_step(i, top):
        for q in range(3):
            plane = jnp.abs(vp[q, VH + i])
            top = jnp.maximum(top, plane)
        return top

    top = lax.fori_loop(0, cx, peak_step, jnp.zeros((ny, nz), jnp.float32))
    tile = top[0:8]
    for row in range(8, ny, 8):
        tile = jnp.maximum(tile, top[row : row + 8])
    mx[me] = tile

    def peak_copy(d):
        return pltpu.make_async_remote_copy(
            src_ref=mx.at[me], dst_ref=mx.at[me],
            send_sem=bar_send.at[d], recv_sem=bar_recv.at[d],
            device_id={"gx": lax.rem(me + d, n)}, device_id_type=MESH,
        )

    def peak_send(d, carry):
        peak_copy(d).start()
        return carry

    lax.fori_loop(1, n, peak_send, 0)

    def spread(which):
        held = lists[which]
        cut, count = held[0:1], held[10:11]
        code = lax.shift_left(jnp.ones_like(cut), held[1:2])
        for k in range(2, 10):
            code = code + lax.shift_left(jnp.ones_like(cut), held[k : k + 1])
        live = lax.broadcasted_iota(jnp.int32, cut.shape, 1) < count
        row = jnp.where(live, lax.shift_right_logical(cut, jnp.full_like(cut, shift_z)), -1)
        z_at = jnp.bitwise_and(cut, nz - 1)
        hit = lax.broadcasted_iota(jnp.int32, (nz, slots), 0) == z_at
        for piece in range(4):
            part = jnp.bitwise_and(
                lax.shift_right_logical(code, jnp.full_like(code, 8 * piece)), 255
            ).astype(jnp.float32)
            spread_t[piece * nz : (piece + 1) * nz] = jnp.where(hit, part, 0.0).astype(jnp.bfloat16)
        return row

    def masks(row, begin, rows):
        at = lax.broadcasted_iota(jnp.int32, (rows, slots), 0) + begin
        chosen = jnp.where(at == row, 1.0, 0.0).astype(jnp.bfloat16)
        out = lax.dot_general(
            chosen, spread_t[...], (((1,), (1,)), ((), ())), preferred_element_type=jnp.float32
        )
        total = out[:, 0:nz].astype(jnp.int32)
        for piece in range(1, 4):
            total = total + out[:, piece * nz : (piece + 1) * nz].astype(jnp.int32) * (1 << (8 * piece))
        return total

    loads[2].wait()
    row = spread(0)
    group = 4 if cx % 4 == 0 else 1

    def mask_step(i, carry):
        part = masks(row, i * (group * ny), group * ny)
        for k in range(group):
            mask_ref[1 + i * group + k] = part[k * ny : (k + 1) * ny]
        return carry

    lax.fori_loop(0, cx // group, mask_step, 0)

    def fraction_step(i):
        fraction = 0.25 * vfp[i].astype(jnp.float32) + 0.25
        for dy in range(3):
            base = roll(fraction, 1 - dy, 0)
            for dz in range(3):
                frr[dy * 3 + dz, i] = roll(base, 1 - dz, 1)

    def fraction_body(i, carry):
        fraction_step(i)
        return carry

    loads[1].wait()
    lax.fori_loop(FH, FH + cx, fraction_body, 0)
    for copy in first:
        copy.wait()
    lax.fori_loop(0, FH, fraction_body, 0)
    lax.fori_loop(FH + cx, FH + cx + FH, fraction_body, 0)
    row = spread(1)
    mask_ref[0] = masks(row, (cx - 1) * ny, ny)
    row = spread(2)
    mask_ref[cx + 1] = masks(row, 0, ny)

    def x_slope(q, i):
        here = vp[q, i]
        return minmod(here - vp[q, i - 1], vp[q, i + 1] - here)

    def x_face(i, q_slopes):
        speed = 0.5 * (vp[0, i] + vp[0, i + 1])
        rate = jnp.minimum(frr[4, i - 1], frr[4, i]) * speed
        ahead = speed > 0
        fluxes = []
        for q in range(3):
            below, above = q_slopes[q]
            fluxes.append(
                rate * jnp.where(ahead, vp[q, i] + 0.5 * below, vp[q, i + 1] - 0.5 * above)
            )
        return fluxes

    start = [(x_slope(q, 1), x_slope(q, 2)) for q in range(3)]
    for q, flux in enumerate(x_face(1, start)):
        fx[q] = flux
        sx[q] = start[q][1]

    lane = lanes((ny, nz))

    def balance_step(s, carry):
        i = s + 2
        pairs = [(sx[q], x_slope(q, i + 1)) for q in range(3)]
        upper = x_face(i, pairs)
        fraction = frr[4, i - 1]
        y_speed = 0.5 * (vp[1, i] + roll(vp[1, i], -1, 0))
        y_rate = jnp.minimum(fraction, frr[7, i - 1]) * y_speed
        z_speed = 0.5 * (vp[2, i] + roll(vp[2, i], -1, 1))
        z_rate = jnp.where(lane == nz - 1, 0.0, jnp.minimum(fraction, frr[5, i - 1]) * z_speed)
        inner = jnp.logical_and(lane > 0, lane < nz - 1)
        held = mask_ref[s]
        hood = jnp.zeros((ny, nz), jnp.float32)
        for dx in range(3):
            for k in range(9):
                hood = hood + jnp.where(
                    jnp.bitwise_and(held, 1 << (dx * 9 + k)) != 0, frr[k, i - 2 + dx], 0.0
                )
        scale = 1.0 / jnp.where(held != 0, hood, 1.0)
        for q in range(3):
            value = vp[q, i]
            result = upper[q] - fx[q]
            fx[q] = upper[q]
            sx[q] = pairs[q][1]
            for axis, speed, rate in ((0, y_speed, y_rate), (1, z_speed, z_rate)):
                ahead_value = roll(value, -1, axis)
                slope = minmod(value - roll(value, 1, axis), ahead_value - value)
                if axis == 1:
                    slope = jnp.where(inner, slope, 0.0)
                flux = rate * jnp.where(
                    speed > 0, value + 0.5 * slope, roll(value - 0.5 * slope, -1, axis)
                )
                result = result + (flux - roll(flux, 1, axis))
            bal[q, s] = result
            amt[q, s] = result * scale
        return carry

    lax.fori_loop(0, cx + 2, balance_step, 0)

    def clear(s, carry):
        for q in range(3):
            moved[q, s] = jnp.zeros((ny, nz), jnp.float32)
        return carry

    lax.fori_loop(0, cx + 4, clear, 0)

    def move_step(s, carry):
        for dy in range(3):
            held = roll(mask_ref[s], dy - 1, 0)
            values = [roll(amt[q, s], dy - 1, 0) for q in range(3)]
            for dz in range(3):
                mask_ref[cx + 2 + dy * 3 + dz] = roll(held, dz - 1, 1)
                for q in range(3):
                    rolled[q, dy * 3 + dz] = roll(values[q], dz - 1, 1)
        for dx in range(3):
            sums = [moved[q, s + dx] for q in range(3)]
            for k in range(9):
                chosen = jnp.bitwise_and(mask_ref[cx + 2 + k], 1 << (dx * 9 + k)) != 0
                for q in range(3):
                    sums[q] = sums[q] + jnp.where(chosen, rolled[q, k], 0.0)
            for q in range(3):
                moved[q, s + dx] = sums[q]
        return carry

    lax.fori_loop(0, cx + 2, move_step, 0)

    def peak_wait(d, carry):
        peak_copy(d).wait()
        return carry

    lax.fori_loop(1, n, peak_wait, 0)
    peak = jnp.max(jnp.max(mx[...], axis=0))
    timestep = COURANT / (peak + 1e-06)

    def advance_step(x, carry):
        keep = jnp.where(mask_ref[x + 1] != 0, 0.0, 1.0 / frr[4, x + FH])
        for q in range(3):
            proj_ref[q, x] = vp[q, x + VH] - timestep * (
                bal[q, x + 1] * keep + moved[q, x + 2]
            )
        return carry

    lax.fori_loop(0, cx, advance_step, 0)

    def source_step(x, carry):
        v, w = proj_ref[1, x], proj_ref[2, x]
        w_up = jnp.where(lane == nz - 1, 0.0, roll(w, -1, 1))
        w_down = jnp.where(lane == 0, 0.0, roll(w, 1, 1))
        f0[PAD + x] = 0.5 * ((roll(v, -1, 0) - roll(v, 1, 0)) + (w_up - w_down))
        return carry

    def source_x(x, carry):
        f0[PAD + x] = f0[PAD + x] + 0.5 * (proj_ref[0, x + 1] - proj_ref[0, x - 1])
        return carry

    lax.fori_loop(0, cx, source_step, 0)
    lax.fori_loop(1, cx - 1, source_x, 0)
    f0[PAD] = f0[PAD] + 0.5 * proj_ref[0, 1]
    f0[PAD + cx - 1] = f0[PAD + cx - 1] - 0.5 * proj_ref[0, cx - 2]
    u_halo[0] = proj_ref[0, 0]
    u_halo[1] = proj_ref[0, cx - 1]
    copies = [
        send(f0.at[PAD + cx - SH : PAD + cx], f0.at[PAD - SH : PAD], right),
        send(f0.at[PAD : PAD + SH], f0.at[PAD + cx : PAD + cx + SH], left),
        send(u_halo.at[1], u_halo.at[2], right),
        send(u_halo.at[0], u_halo.at[3], left),
    ]
    for copy in copies:
        copy.wait()
    f0[PAD] = f0[PAD] - 0.5 * u_halo[2]
    f0[PAD + cx - 1] = f0[PAD + cx - 1] + 0.5 * u_halo[3]
    f0[PAD - 1] = f0[PAD - 1] + 0.5 * u_halo[0]
    f0[PAD + cx] = f0[PAD + cx] - 0.5 * u_halo[1]

    chunks = (2, 2, 0)

    def over(level, low, high, body):
        step = chunks[level]
        if step == 0:
            body(PAD + low, high - low)
        else:
            def run(i, carry):
                body(PAD + low + i * step, step)
                return carry
            lax.fori_loop(0, (high - low) // step, run, 0)

    def around(src, at, size, level):
        here = src[pl.ds(at, size)]
        lane_at = lanes(here.shape)
        hop = 1 << level
        z_up = jnp.where(lane_at >= nz - hop, here, roll(here, -hop, 2))
        z_down = jnp.where(lane_at < hop, here, roll(here, hop, 2))
        nbsum = (
            (src[pl.ds(at + 1, size)] + src[pl.ds(at - 1, size)])
            + (roll(here, -1, 1) + roll(here, 1, 1))
            + (z_up + z_down)
        )
        return here, nbsum

    def seed(dst, f, level, low, high):
        def body(at, size):
            dst[pl.ds(at, size)] = (-WEIGHT * 4.0**level) * f[pl.ds(at, size)]
        over(level, low, high, body)

    def sweep(src, dst, f, level, low, high):
        def body(at, size):
            here, nbsum = around(src, at, size, level)
            dst[pl.ds(at, size)] = (1.0 - DAMP) * here + WEIGHT * (
                nbsum - (4.0**level) * f[pl.ds(at, size)]
            )
        over(level, low, high, body)

    def restrict(src, f, coarse, level, low, high, scratch):
        rows = f.shape[1]

        def body(i, carry):
            at = PAD + 2 * (low + i)
            here, nbsum = around(src, at, 2, level)
            residue = f[pl.ds(at, 2)] - (nbsum - 6.0 * here) * (1.0 / 4.0**level)
            scratch[...] = residue[0] + residue[1]
            pair = scratch[pl.ds(0, rows // 2, stride=2), :] + scratch[pl.ds(1, rows // 2, stride=2), :]
            lane_at = lanes(pair.shape)
            hop = 1 << level
            other = jnp.where(
                jnp.bitwise_and(lane_at, hop) == 0, roll(pair, -hop, 1), roll(pair, hop, 1)
            )
            coarse[PAD + low + i] = 0.125 * (pair + other)
            return carry

        lax.fori_loop(0, high - low, body, 0)

    def correct(p, coarse, low, high, scratch):
        rows = p.shape[1]

        def body(i, carry):
            value = coarse[PAD + low + i]
            scratch[pl.ds(0, rows // 2, stride=2), :] = value
            scratch[pl.ds(1, rows // 2, stride=2), :] = value
            at = PAD + 2 * (low + i)
            fine = scratch[...]
            p[at] = p[at] + fine
            p[at + 1] = p[at + 1] + fine
            return carry

        lax.fori_loop(0, high - low, body, 0)

    def planes_in(dst, land, begin, size):
        dst[begin : begin + size] = land[...]

    c1, c2 = cx // 2, cx // 4
    for cycle in range(CYCLES):
        if cycle == 0:
            seed(p0a, f0, 0, -4, cx + 4)
        else:
            copies = [
                send(p0a.at[cx : PAD + cx], land0.at[0], right),
                send(p0a.at[PAD : 2 * PAD], land0.at[1], left),
            ]
            for copy in copies:
                copy.wait()
            planes_in(p0a, land0.at[0], 0, PAD)
            planes_in(p0a, land0.at[1], PAD + cx, PAD)
            sweep(p0a, p0b, f0, 0, -4, cx + 4)
        before, after = (p0a, p0b) if cycle == 0 else (p0b, p0a)
        sweep(before, after, f0, 0, -3, cx + 3)
        restrict(after, f0, f1, 0, 0, c1, tmp)
        copies = [
            send(f1.at[c1 : PAD + c1], land1.at[cycle, 0], right),
            send(f1.at[PAD : 2 * PAD], land1.at[cycle, 1], left),
        ]
        for copy in copies:
            copy.wait()
        planes_in(f1, land1.at[cycle, 0], 0, PAD)
        planes_in(f1, land1.at[cycle, 1], PAD + c1, PAD)
        seed(p1a, f1, 1, -5, c1 + 5)
        sweep(p1a, p1b, f1, 1, -4, c1 + 4)
        restrict(p1b, f1, f2, 1, -1, c2 + 1, tmp1)
        copies = [
            send(f2.at[c2 - 1 + PAD - 4 : PAD + c2], land2.at[cycle, 0], right),
            send(f2.at[PAD : 2 * PAD], land2.at[cycle, 1], left),
        ]
        for copy in copies:
            copy.wait()
        planes_in(f2, land2.at[cycle, 0], 0, PAD)
        planes_in(f2, land2.at[cycle, 1], PAD + c2, PAD)
        seed(p2a, f2, 2, -5, c2 + 5)
        sweep(p2a, p2b, f2, 2, -4, c2 + 4)
        sweep(p2b, p2a, f2, 2, -3, c2 + 3)
        sweep(p2a, p2b, f2, 2, -2, c2 + 2)
        correct(p1b, p2b, -2, c2 + 2, tmp1)
        sweep(p1b, p1a, f1, 1, -3, c1 + 3)
        sweep(p1a, p1b, f1, 1, -2, c1 + 2)
        correct(after, p1b, -2, c1 + 2, tmp)
        sweep(after, before, f0, 0, -2, cx + 2)
        sweep(before, after, f0, 0, -1, cx + 1)
        if cycle == 0:
            p0a, p0b = after, before

    final = after

    def project_step(x, carry):
        here = final[PAD + x]
        pot_ref[x] = here
        proj_ref[0, x] = proj_ref[0, x] - 0.5 * (final[PAD + x + 1] - final[PAD + x - 1])
        proj_ref[1, x] = proj_ref[1, x] - 0.5 * (roll(here, -1, 0) - roll(here, 1, 0))
        z_up = jnp.where(lane == nz - 1, here, roll(here, -1, 1))
        z_down = jnp.where(lane == 0, here, roll(here, 1, 1))
        proj_ref[2, x] = proj_ref[2, x] - 0.5 * (z_up - z_down)
        return carry

    lax.fori_loop(0, cx, project_step, 0)


def local(n, velocity, vfrac_class, cut_cells, cut_count, offsets):
    cx, ny, nz = vfrac_class.shape
    slots = cut_cells.shape[0]
    hood = offsets.shape[0]
    lists = jnp.concatenate(
        [
            cut_cells[None],
            offsets,
            jnp.broadcast_to(cut_count[:, None], (16 - 1 - hood, slots)),
        ]
    )
    f32 = jnp.float32
    vm = pltpu.VMEM
    level = lambda l: vm((cx // 2**l + 2 * PAD, ny // 2**l, nz), f32)
    return tuple(
        pl.pallas_call(
            functools.partial(kernel, n),
            out_shape=(
                jax.ShapeDtypeStruct(velocity.shape, f32),
                jax.ShapeDtypeStruct(vfrac_class.shape, f32),
            ),
            in_specs=[pl.BlockSpec(memory_space=pl.ANY)] * 3,
            out_specs=(pl.BlockSpec(memory_space=pltpu.VMEM),) * 2,
            scratch_shapes=[
                vm((3, cx + 2 * VH, ny, nz), f32),
                vm((cx + 2 * FH, ny, nz), jnp.int32),
                vm((3, 16, slots), jnp.int32),
                vm((n, 8, nz), f32),
                vm((9, cx + 2 * FH, ny, nz), f32),
                vm((cx + 2 + 9, ny, nz), jnp.int32),
                vm((3, cx + 2, ny, nz), f32),
                vm((3, cx + 2, ny, nz), f32),
                vm((3, cx + 4, ny, nz), f32),
                vm((3, 9, ny, nz), f32),
                vm((3, ny, nz), f32),
                vm((3, ny, nz), f32),
                vm((4 * nz, slots), jnp.bfloat16),
                vm((4, ny, nz), f32),
                level(0), level(0), level(0), vm((2, PAD, ny, nz), f32),
                level(1), level(1), level(1), vm((CYCLES, 2, PAD, ny // 2, nz), f32),
                level(2), level(2), level(2), vm((CYCLES, 2, PAD, ny // 4, nz), f32),
                vm((ny, nz), f32),
                vm((ny // 2, nz), f32),
                pltpu.SemaphoreType.DMA((n,)),
                pltpu.SemaphoreType.DMA((n,)),
                pltpu.SemaphoreType.DMA((3,)),
                pltpu.SemaphoreType.DMA((20,)),
                pltpu.SemaphoreType.DMA((20,)),
            ],
            compiler_params=pltpu.CompilerParams(
                collective_id=0, has_side_effects=True, vmem_limit_bytes=48 * 2**20
            ),
        )(velocity, vfrac_class, lists)
    )


def solution(mesh):
    placed = (
        P("grp", "gx", None, None),
        P(("grp", "gx"), None, None),
        P(("grp", "gx")),
        P(("grp", "gx")),
        P("grp", "gx"),
    )
    return jax.shard_map(
        functools.partial(local, mesh.shape["gx"]),
        mesh=mesh,
        in_specs=placed,
        out_specs=(P("grp", "gx", None, None), P(("grp", "gx"), None, None)),
        check_vma=False,
    )
```

time: 787 us -> 85.8 us (0.11)
  local copies, waits for them, and re-layouts: 344 us -> 4.46 us
  other arithmetic: 226 us -> 0.92 us
  starting transfers between devices: 129 us -> 0 us
  Pallas kernels: 0 us -> 78.9 us
  waiting for transfers between devices: 42.3 us -> 0 us
  blocking collectives: 35 us -> 0 us
    scatter-add x6 -> x0, other arithmetic: 153 us -> none  [the longest x3 145 us: local(): jnp.zeros((3, (x_cells + 2) * y_cells * z_cells), jnp.float32).at[:, place]]
    ppermute x62 -> x0, starting transfers between devices: 129 us -> none  [the longest x30 126 us: with_halo(): lax.ppermute(lax.slice_in_dim(block, 0, width, axis=dim), axis, backward)]
    gather x4 -> x0, local copies, waits for them, and re-layouts: 84.7 us -> none  [the longest x2 74 us: local(): fraction_xpad[0, x_target + 2, y_target, z_target]]
    reshape x16 -> x0, local copies, waits for them, and re-layouts: 84.6 us -> none  [the longest x4 81.2 us: restrict_field(): values.reshape(x_size // 2, 2, y_size // 2, 2, z_size // 2, 2)]
    pallas_call x0 -> x1, Pallas kernels: none -> 78.9 us  [local(): pl.pallas_call(functools.partial(kernel, n), out_shape=(jax.ShapeDtypeStr...]
    slice x114 -> x0, local copies, waits for them, and re-layouts: 78 us -> none  [the longest x1 44.1 us: local(): moved = widened[:, 1:-1].at[:, -1].add(from_next).at[:, 0].add(from_prior)]
    unnamed x64 -> x6, local copies, waits for them, and re-layouts: 56.2 us -> 4.39 us
    ppermute x62 -> x0, waiting for transfers between devices: 42.3 us -> none  [the longest x30 35.3 us: with_halo(): lax.ppermute(lax.slice_in_dim(block, block.shape[dim] - width, None, axis...]
  transfers between devices with their start and end apart: 62 -> 0, of which waited for: 42 -> 0; matrix products, arithmetic and copies ran while one was open for 64% -> 0% of each run, Pallas kernels for 0% -> 0%
where the time goes in v1:
time: 85.8 us; the launch traced here: 85.5 us
  Pallas kernels  78.9 us (92%)
  local copies, waits for them, and re-layouts  4.46 us (5%)
  between operations  1.3 us (2%)
  other arithmetic  0.92 us (1%)
    pallas_call x1, Pallas kernels, local(): pl.pallas_call(functools.partial(kernel, n), out_shape=(jax.ShapeDtypeStr...  78.9 us
    unnamed x6, local copies, waits for them, and re-layouts  4.39 us

profile of v1, /device:TPU:0, one launch (start us, length us, event | category | flops | bytes accessed | tf_op | source)
XLA Modules:
  0.0 85.5 jit_solution(11944305798027952577)
XLA Ops:
  1.3 0.1 pad.2.clone
  1.4 0.9 %add_add_fusion.lists_hbm = s32[16,1024]{1,0:T(8,128)S(1)} fusion(s32[9,1024]{1,0:T(8,128)} %param.9, s32[1,1024]{1,0:T(1,128)} %bitcast.3, s32[16]{0:T(128)S(1)} %pad.2.clone), kind=kLoop, calls=%fused_computation | loop fusion | flops 32768 | bytes 106560 | tf_op jit(solution)/shard_map/concatenate | solution.py:454
  2.3 0.0 copy-start
  2.3 1.4 %copy-done = f32[3,16,64,128]{3,2,1,0:T(8,128)S(1)} copy-done((f32[3,16,64,128]{3,2,1,0:T(8,128)S(1)}, f32[3,16,64,128]{3,2,1,0:T(8,128)}, u32[]{:S(2)}) %copy-start) | copy-done | bytes 1572888
  3.7 0.0 copy-start.1
  3.7 1.0 %copy-done.1 = s32[16,64,128]{2,1,0:T(8,128)S(1)} copy-done((s32[16,64,128]{2,1,0:T(8,128)S(1)}, s32[16,64,128]{2,1,0:T(8,128)}, u32[]{:S(2)}) %copy-start.1) | copy-done | bytes 524312
  4.7 78.9 %shard_map.68 = (f32[3,16,64,128]{3,2,1,0:T(8,128)S(1)}, f32[16,64,128]{2,1,0:T(8,128)S(1)}) custom-call(f32[3,16,64,128]{3,2,1,0:T(8,128)S(1)} %copy-done, s32[16,64,128]{2,1,0:T(8,128)S(1)} %copy-done.1, s32[16,1024]{1,0:T(8,128)S(1)} %add_add_fusion.lists_hbm), custom_call_target="tpu_custom_call" | custom-call | tf_op jit(solution)/shard_map/pallas_call | solution.py:465
  83.6 1.1 %copy.10 = f32[3,16,64,128]{3,2,1,0:T(8,128)} copy(f32[3,16,64,128]{3,2,1,0:T(8,128)S(1)} %get-tuple-element.4) | data formatting | bytes 3145728
  84.7 0.8 copy.11
  (1 shorter events, 0.0 us)
Async XLA Ops:
  2.3 1.4 %copy-start = (f32[3,16,64,128]{3,2,1,0:T(8,128)S(1)}, f32[3,16,64,128]{3,2,1,0:T(8,128)}, u32[]{:S(2)}) copy-start(f32[3,16,64,128]{3,2,1,0:T(8,128)} %vel_hbm.1) | copy-start | bytes 4718596
  3.7 1.0 %copy-start.1 = (s32[16,64,128]{2,1,0:T(8,128)S(1)}, s32[16,64,128]{2,1,0:T(8,128)}, u32[]{:S(2)}) copy-start(s32[16,64,128]{2,1,0:T(8,128)} %vf_hbm.1) | copy-start | bytes 1572868

commit v2 on v1

--- a/solution.py
+++ b/solution.py
@@ -27,6 +27,18 @@
     return lax.broadcasted_iota(jnp.int32, shape, len(shape) - 1)
 
 
+def planes(low, high, turns, body):
+    def run(i, carry):
+        for k in range(turns):
+            body(low + i * turns + k)
+        return carry
+
+    count = (high - low) // turns
+    lax.fori_loop(0, count, run, 0)
+    for at in range(low + count * turns, high):
+        body(at)
+
+
 def minmod(a, b):
     return jnp.maximum(jnp.minimum(a, b), 0.0) + jnp.minimum(jnp.maximum(a, b), 0.0)
 
@@ -34,7 +46,7 @@
 def kernel(
     n, vel_hbm, vf_hbm, lists_hbm, proj_ref, pot_ref,
     vp, vfp, lists, mx, frr, mask_ref, bal, amt, moved, rolled, fx, sx, spread_t,
-    u_halo, f0, p0a, p0b, land0, f1, p1a, p1b, land1, f2, p2a, p2b, land2, tmp, tmp1,
+    u_halo, f0, p0a, p0b, p0c, land0, f1, p1a, p1b, land1, f2, p2a, p2b, land2, tmp, tmp1,
     bar_send, bar_recv, load_sem, send_sem, recv_sem,
 ):
     me = lax.axis_index("gx")
@@ -157,20 +169,8 @@
             for dz in range(3):
                 frr[dy * 3 + dz, i] = roll(base, 1 - dz, 1)
 
-    def fraction_body(i, carry):
-        fraction_step(i)
-        return carry
-
     loads[1].wait()
-    lax.fori_loop(FH, FH + cx, fraction_body, 0)
-    for copy in first:
-        copy.wait()
-    lax.fori_loop(0, FH, fraction_body, 0)
-    lax.fori_loop(FH + cx, FH + cx + FH, fraction_body, 0)
-    row = spread(1)
-    mask_ref[0] = masks(row, (cx - 1) * ny, ny)
-    row = spread(2)
-    mask_ref[cx + 1] = masks(row, 0, ny)
+    planes(FH, FH + cx, 2, fraction_step)
 
     def x_slope(q, i):
         here = vp[q, i]
@@ -187,11 +187,6 @@
                 rate * jnp.where(ahead, vp[q, i] + 0.5 * below, vp[q, i + 1] - 0.5 * above)
             )
         return fluxes
-
-    start = [(x_slope(q, 1), x_slope(q, 2)) for q in range(3)]
-    for q, flux in enumerate(x_face(1, start)):
-        fx[q] = flux
-        sx[q] = start[q][1]
 
     lane = lanes((ny, nz))
 
@@ -231,7 +226,24 @@
             amt[q, s] = result * scale
         return carry
 
-    lax.fori_loop(0, cx + 2, balance_step, 0)
+    def balance_planes(low, high):
+        begin = [(x_slope(q, low + 1), x_slope(q, low + 2)) for q in range(3)]
+        for q, flux in enumerate(x_face(low + 1, begin)):
+            fx[q] = flux
+            sx[q] = begin[q][1]
+        lax.fori_loop(low, high, balance_step, 0)
+
+    balance_planes(3, cx - 1)
+    for copy in first:
+        copy.wait()
+    planes(0, FH, 2, fraction_step)
+    planes(FH + cx, FH + cx + FH, 2, fraction_step)
+    row = spread(1)
+    mask_ref[0] = masks(row, (cx - 1) * ny, ny)
+    row = spread(2)
+    mask_ref[cx + 1] = masks(row, 0, ny)
+    balance_planes(0, 3)
+    balance_planes(cx - 1, cx + 2)
 
     def clear(s, carry):
         for q in range(3):
@@ -268,29 +280,26 @@
     peak = jnp.max(jnp.max(mx[...], axis=0))
     timestep = COURANT / (peak + 1e-06)
 
-    def advance_step(x, carry):
+    def advance_step(x):
         keep = jnp.where(mask_ref[x + 1] != 0, 0.0, 1.0 / frr[4, x + FH])
         for q in range(3):
             proj_ref[q, x] = vp[q, x + VH] - timestep * (
                 bal[q, x + 1] * keep + moved[q, x + 2]
             )
-        return carry
-
-    lax.fori_loop(0, cx, advance_step, 0)
-
-    def source_step(x, carry):
+
+    planes(0, cx, 2, advance_step)
+
+    def source_step(x):
         v, w = proj_ref[1, x], proj_ref[2, x]
         w_up = jnp.where(lane == nz - 1, 0.0, roll(w, -1, 1))
         w_down = jnp.where(lane == 0, 0.0, roll(w, 1, 1))
         f0[PAD + x] = 0.5 * ((roll(v, -1, 0) - roll(v, 1, 0)) + (w_up - w_down))
-        return carry
-
-    def source_x(x, carry):
+
+    def source_x(x):
         f0[PAD + x] = f0[PAD + x] + 0.5 * (proj_ref[0, x + 1] - proj_ref[0, x - 1])
-        return carry
-
-    lax.fori_loop(0, cx, source_step, 0)
-    lax.fori_loop(1, cx - 1, source_x, 0)
+
+    planes(0, cx, 4, source_step)
+    planes(1, cx - 1, 7, source_x)
     f0[PAD] = f0[PAD] + 0.5 * proj_ref[0, 1]
     f0[PAD + cx - 1] = f0[PAD + cx - 1] - 0.5 * proj_ref[0, cx - 2]
     u_halo[0] = proj_ref[0, 0]
@@ -301,14 +310,14 @@
         send(u_halo.at[1], u_halo.at[2], right),
         send(u_halo.at[0], u_halo.at[3], left),
     ]
-    for copy in copies:
-        copy.wait()
-    f0[PAD] = f0[PAD] - 0.5 * u_halo[2]
-    f0[PAD + cx - 1] = f0[PAD + cx - 1] + 0.5 * u_halo[3]
-    f0[PAD - 1] = f0[PAD - 1] + 0.5 * u_halo[0]
-    f0[PAD + cx] = f0[PAD + cx] - 0.5 * u_halo[1]
-
-    chunks = (2, 2, 0)
+
+    def finish_source():
+        f0[PAD] = f0[PAD] - 0.5 * u_halo[2]
+        f0[PAD + cx - 1] = f0[PAD + cx - 1] + 0.5 * u_halo[3]
+        f0[PAD - 1] = f0[PAD - 1] + 0.5 * u_halo[0]
+        f0[PAD + cx] = f0[PAD + cx] - 0.5 * u_halo[1]
+
+    chunks = (8, 0, 0)
 
     def over(level, low, high, body):
         step = chunks[level]
@@ -318,7 +327,11 @@
             def run(i, carry):
                 body(PAD + low + i * step, step)
                 return carry
-            lax.fori_loop(0, (high - low) // step, run, 0)
+            count = (high - low) // step
+            lax.fori_loop(0, count, run, 0)
+            rest = high - low - count * step
+            if rest:
+                body(PAD + low + count * step, rest)
 
     def around(src, at, size, level):
         here = src[pl.ds(at, size)]
@@ -346,39 +359,49 @@
             )
         over(level, low, high, body)
 
+    def unrolled(count, body, turns):
+        def run(i, carry):
+            for k in range(turns):
+                body(i * turns + k, k)
+            return carry
+
+        lax.fori_loop(0, count // turns, run, 0)
+        for k in range(count % turns):
+            body(count // turns * turns + k, k)
+
     def restrict(src, f, coarse, level, low, high, scratch):
         rows = f.shape[1]
 
-        def body(i, carry):
+        def body(i, slot):
+            held = scratch.at[slot]
             at = PAD + 2 * (low + i)
             here, nbsum = around(src, at, 2, level)
             residue = f[pl.ds(at, 2)] - (nbsum - 6.0 * here) * (1.0 / 4.0**level)
-            scratch[...] = residue[0] + residue[1]
-            pair = scratch[pl.ds(0, rows // 2, stride=2), :] + scratch[pl.ds(1, rows // 2, stride=2), :]
+            held[...] = residue[0] + residue[1]
+            pair = held[pl.ds(0, rows // 2, stride=2), :] + held[pl.ds(1, rows // 2, stride=2), :]
             lane_at = lanes(pair.shape)
             hop = 1 << level
             other = jnp.where(
                 jnp.bitwise_and(lane_at, hop) == 0, roll(pair, -hop, 1), roll(pair, hop, 1)
             )
             coarse[PAD + low + i] = 0.125 * (pair + other)
-            return carry
-
-        lax.fori_loop(0, high - low, body, 0)
+
+        unrolled(high - low, body, scratch.shape[0])
 
     def correct(p, coarse, low, high, scratch):
         rows = p.shape[1]
 
-        def body(i, carry):
+        def body(i, slot):
+            held = scratch.at[slot]
             value = coarse[PAD + low + i]
-            scratch[pl.ds(0, rows // 2, stride=2), :] = value
-            scratch[pl.ds(1, rows // 2, stride=2), :] = value
+            held[pl.ds(0, rows // 2, stride=2), :] = value
+            held[pl.ds(1, rows // 2, stride=2), :] = value
             at = PAD + 2 * (low + i)
-            fine = scratch[...]
+            fine = held[...]
             p[at] = p[at] + fine
             p[at + 1] = p[at + 1] + fine
-            return carry
-
-        lax.fori_loop(0, high - low, body, 0)
+
+        unrolled(high - low, body, scratch.shape[0])
 
     def planes_in(dst, land, begin, size):
         dst[begin : begin + size] = land[...]
@@ -386,30 +409,46 @@
     c1, c2 = cx // 2, cx // 4
     for cycle in range(CYCLES):
         if cycle == 0:
-            seed(p0a, f0, 0, -4, cx + 4)
+            before, after = p0a, p0b
+            seed(before, f0, 0, 1, cx - 1)
         else:
             copies = [
                 send(p0a.at[cx : PAD + cx], land0.at[0], right),
                 send(p0a.at[PAD : 2 * PAD], land0.at[1], left),
             ]
-            for copy in copies:
-                copy.wait()
+            before, after = p0b, p0c
+            sweep(p0a, before, f0, 0, 1, cx - 1)
+        sweep(before, after, f0, 0, 2, cx - 2)
+        restrict(after, f0, f1, 0, 2, c1 - 2, tmp)
+        for copy in copies:
+            copy.wait()
+        if cycle == 0:
+            finish_source()
+            seed(before, f0, 0, -4, 1)
+            seed(before, f0, 0, cx - 1, cx + 4)
+        else:
             planes_in(p0a, land0.at[0], 0, PAD)
             planes_in(p0a, land0.at[1], PAD + cx, PAD)
-            sweep(p0a, p0b, f0, 0, -4, cx + 4)
-        before, after = (p0a, p0b) if cycle == 0 else (p0b, p0a)
-        sweep(before, after, f0, 0, -3, cx + 3)
-        restrict(after, f0, f1, 0, 0, c1, tmp)
+            sweep(p0a, before, f0, 0, -4, 1)
+            sweep(p0a, before, f0, 0, cx - 1, cx + 4)
+        sweep(before, after, f0, 0, -3, 2)
+        sweep(before, after, f0, 0, cx - 2, cx + 3)
+        restrict(after, f0, f1, 0, 0, 2, tmp)
+        restrict(after, f0, f1, 0, c1 - 2, c1, tmp)
         copies = [
             send(f1.at[c1 : PAD + c1], land1.at[cycle, 0], right),
             send(f1.at[PAD : 2 * PAD], land1.at[cycle, 1], left),
         ]
+        seed(p1a, f1, 1, 0, c1)
+        sweep(p1a, p1b, f1, 1, 1, c1 - 1)
         for copy in copies:
             copy.wait()
         planes_in(f1, land1.at[cycle, 0], 0, PAD)
         planes_in(f1, land1.at[cycle, 1], PAD + c1, PAD)
-        seed(p1a, f1, 1, -5, c1 + 5)
-        sweep(p1a, p1b, f1, 1, -4, c1 + 4)
+        seed(p1a, f1, 1, -5, 0)
+        seed(p1a, f1, 1, c1, c1 + 5)
+        sweep(p1a, p1b, f1, 1, -4, 1)
+        sweep(p1a, p1b, f1, 1, c1 - 1, c1 + 4)
         restrict(p1b, f1, f2, 1, -1, c2 + 1, tmp1)
         copies = [
             send(f2.at[c2 - 1 + PAD - 4 : PAD + c2], land2.at[cycle, 0], right),
@@ -434,7 +473,7 @@
 
     final = after
 
-    def project_step(x, carry):
+    def project_step(x):
         here = final[PAD + x]
         pot_ref[x] = here
         proj_ref[0, x] = proj_ref[0, x] - 0.5 * (final[PAD + x + 1] - final[PAD + x - 1])
@@ -442,9 +481,8 @@
         z_up = jnp.where(lane == nz - 1, here, roll(here, -1, 1))
         z_down = jnp.where(lane == 0, here, roll(here, 1, 1))
         proj_ref[2, x] = proj_ref[2, x] - 0.5 * (z_up - z_down)
-        return carry
-
-    lax.fori_loop(0, cx, project_step, 0)
+
+    planes(0, cx, 4, project_step)
 
 
 def local(n, velocity, vfrac_class, cut_cells, cut_count, offsets):
@@ -485,11 +523,11 @@
                 vm((3, ny, nz), f32),
                 vm((4 * nz, slots), jnp.bfloat16),
                 vm((4, ny, nz), f32),
-                level(0), level(0), level(0), vm((2, PAD, ny, nz), f32),
+                level(0), level(0), level(0), level(0), vm((2, PAD, ny, nz), f32),
                 level(1), level(1), level(1), vm((CYCLES, 2, PAD, ny // 2, nz), f32),
                 level(2), level(2), level(2), vm((CYCLES, 2, PAD, ny // 4, nz), f32),
-                vm((ny, nz), f32),
-                vm((ny // 2, nz), f32),
+                vm((4, ny, nz), f32),
+                vm((3, ny // 2, nz), f32),
                 pltpu.SemaphoreType.DMA((n,)),
                 pltpu.SemaphoreType.DMA((n,)),
                 pltpu.SemaphoreType.DMA((3,)),

time: 85.8 us -> 68.7 us (0.80)
  Pallas kernels: 78.9 us -> 61.8 us
    pallas_call x1, Pallas kernels: 78.9 us -> 61.8 us  [local(): pl.pallas_call(functools.partial(kernel, n), out_shape=(jax.ShapeDtypeStr...]
where the time goes in v2:
time: 68.7 us; the launch traced here: 68.5 us
  Pallas kernels  61.8 us (90%)
  local copies, waits for them, and re-layouts  4.46 us (6%)
  between operations  1.3 us (2%)
  other arithmetic  0.92 us (1%)
    pallas_call x1, Pallas kernels, local(): pl.pallas_call(functools.partial(kernel, n), out_shape=(jax.ShapeDtypeStr...  61.8 us
    unnamed x6, local copies, waits for them, and re-layouts  4.39 us

profile of v2, /device:TPU:0, one launch (start us, length us, event | category | flops | bytes accessed | tf_op | source)
XLA Modules:
  0.0 68.5 jit_solution(8130713549511659193)
XLA Ops:
  1.3 0.1 pad.2.clone
  1.4 0.9 %add_add_fusion.lists_hbm = s32[16,1024]{1,0:T(8,128)S(1)} fusion(s32[9,1024]{1,0:T(8,128)} %param.9, s32[1,1024]{1,0:T(1,128)} %bitcast.3, s32[16]{0:T(128)S(1)} %pad.2.clone), kind=kLoop, calls=%fused_computation | loop fusion | flops 32768 | bytes 106560 | tf_op jit(solution)/shard_map/concatenate | solution.py:492
  2.3 0.0 copy-start
  2.3 1.4 %copy-done = f32[3,16,64,128]{3,2,1,0:T(8,128)S(1)} copy-done((f32[3,16,64,128]{3,2,1,0:T(8,128)S(1)}, f32[3,16,64,128]{3,2,1,0:T(8,128)}, u32[]{:S(2)}) %copy-start) | copy-done | bytes 1572888
  3.7 0.0 copy-start.1
  3.7 1.0 %copy-done.1 = s32[16,64,128]{2,1,0:T(8,128)S(1)} copy-done((s32[16,64,128]{2,1,0:T(8,128)S(1)}, s32[16,64,128]{2,1,0:T(8,128)}, u32[]{:S(2)}) %copy-start.1) | copy-done | bytes 524312
  4.7 61.8 %shard_map.68 = (f32[3,16,64,128]{3,2,1,0:T(8,128)S(1)}, f32[16,64,128]{2,1,0:T(8,128)S(1)}) custom-call(f32[3,16,64,128]{3,2,1,0:T(8,128)S(1)} %copy-done, s32[16,64,128]{2,1,0:T(8,128)S(1)} %copy-done.1, s32[16,1024]{1,0:T(8,128)S(1)} %add_add_fusion.lists_hbm), custom_call_target="tpu_custom_call" | custom-call | tf_op jit(solution)/shard_map/pallas_call | solution.py:503
  66.5 1.1 %copy.10 = f32[3,16,64,128]{3,2,1,0:T(8,128)} copy(f32[3,16,64,128]{3,2,1,0:T(8,128)S(1)} %get-tuple-element.4) | data formatting | bytes 3145728
  67.7 0.8 %copy.11 = f32[16,64,128]{2,1,0:T(8,128)} copy(f32[16,64,128]{2,1,0:T(8,128)S(1)} %get-tuple-element.5) | data formatting | bytes 1048576
  (1 shorter events, 0.0 us)
Async XLA Ops:
  2.3 1.4 %copy-start = (f32[3,16,64,128]{3,2,1,0:T(8,128)S(1)}, f32[3,16,64,128]{3,2,1,0:T(8,128)}, u32[]{:S(2)}) copy-start(f32[3,16,64,128]{3,2,1,0:T(8,128)} %vel_hbm.1) | copy-start | bytes 4718596
  3.7 1.0 %copy-start.1 = (s32[16,64,128]{2,1,0:T(8,128)S(1)}, s32[16,64,128]{2,1,0:T(8,128)}, u32[]{:S(2)}) copy-start(s32[16,64,128]{2,1,0:T(8,128)} %vf_hbm.1) | copy-start | bytes 1572868

commit v3 on v2

--- a/solution.py
+++ b/solution.py
@@ -287,7 +287,8 @@
                 bal[q, x + 1] * keep + moved[q, x + 2]
             )
 
-    planes(0, cx, 2, advance_step)
+    planes(0, SH + 1, 2, advance_step)
+    planes(cx - SH - 1, cx, 2, advance_step)
 
     def source_step(x):
         v, w = proj_ref[1, x], proj_ref[2, x]
@@ -298,8 +299,10 @@
     def source_x(x):
         f0[PAD + x] = f0[PAD + x] + 0.5 * (proj_ref[0, x + 1] - proj_ref[0, x - 1])
 
-    planes(0, cx, 4, source_step)
-    planes(1, cx - 1, 7, source_x)
+    planes(0, SH, 4, source_step)
+    planes(cx - SH, cx, 4, source_step)
+    planes(1, SH, 3, source_x)
+    planes(cx - SH, cx - 1, 3, source_x)
     f0[PAD] = f0[PAD] + 0.5 * proj_ref[0, 1]
     f0[PAD + cx - 1] = f0[PAD + cx - 1] - 0.5 * proj_ref[0, cx - 2]
     u_halo[0] = proj_ref[0, 0]
@@ -310,6 +313,9 @@
         send(u_halo.at[1], u_halo.at[2], right),
         send(u_halo.at[0], u_halo.at[3], left),
     ]
+    planes(SH + 1, cx - SH - 1, 3, advance_step)
+    planes(SH, cx - SH, 4, source_step)
+    planes(SH, cx - SH, 4, source_x)
 
     def finish_source():
         f0[PAD] = f0[PAD] - 0.5 * u_halo[2]
@@ -412,10 +418,6 @@
             before, after = p0a, p0b
             seed(before, f0, 0, 1, cx - 1)
         else:
-            copies = [
-                send(p0a.at[cx : PAD + cx], land0.at[0], right),
-                send(p0a.at[PAD : 2 * PAD], land0.at[1], left),
-            ]
             before, after = p0b, p0c
             sweep(p0a, before, f0, 0, 1, cx - 1)
         sweep(before, after, f0, 0, 2, cx - 2)
@@ -462,13 +464,22 @@
         sweep(p2a, p2b, f2, 2, -4, c2 + 4)
         sweep(p2b, p2a, f2, 2, -3, c2 + 3)
         sweep(p2a, p2b, f2, 2, -2, c2 + 2)
+        more = 0 if cycle < CYCLES - 1 else 1
         correct(p1b, p2b, -2, c2 + 2, tmp1)
-        sweep(p1b, p1a, f1, 1, -3, c1 + 3)
-        sweep(p1a, p1b, f1, 1, -2, c1 + 2)
-        correct(after, p1b, -2, c1 + 2, tmp)
-        sweep(after, before, f0, 0, -2, cx + 2)
-        sweep(before, after, f0, 0, -1, cx + 1)
-        if cycle == 0:
+        sweep(p1b, p1a, f1, 1, -2 - more, c1 + 2 + more)
+        sweep(p1a, p1b, f1, 1, -1 - more, c1 + 1 + more)
+        correct(after, p1b, -1 - more, c1 + 1 + more, tmp)
+        sweep(after, before, f0, 0, -1 - more, cx + 1 + more)
+        if more:
+            sweep(before, after, f0, 0, -1, cx + 1)
+        else:
+            sweep(before, after, f0, 0, 0, PAD)
+            sweep(before, after, f0, 0, cx - PAD, cx)
+            copies = [
+                send(after.at[cx : PAD + cx], land0.at[0], right),
+                send(after.at[PAD : 2 * PAD], land0.at[1], left),
+            ]
+            sweep(before, after, f0, 0, PAD, cx - PAD)
             p0a, p0b = after, before
 
     final = after

time: 68.7 us -> 67.7 us (0.985)
  Pallas kernels: 61.8 us -> 60.8 us
    pallas_call x1, Pallas kernels: 61.8 us -> 60.8 us  [local(): pl.pallas_call(functools.partial(kernel, n), out_shape=(jax.ShapeDtypeStr...]
where the time goes in v3:
time: 67.7 us; the launch traced here: 67.5 us
  Pallas kernels  60.8 us (90%)
  local copies, waits for them, and re-layouts  4.46 us (7%)
  between operations  1.3 us (2%)
  other arithmetic  0.92 us (1%)
    pallas_call x1, Pallas kernels, local(): pl.pallas_call(functools.partial(kernel, n), out_shape=(jax.ShapeDtypeStr...  60.8 us
    unnamed x6, local copies, waits for them, and re-layouts  4.39 us

profile of v3, /device:TPU:0, one launch (start us, length us, event | category | flops | bytes accessed | tf_op | source)
XLA Modules:
  0.0 67.5 jit_solution(13190022279963550929)
XLA Ops:
  1.3 0.1 pad.2.clone
  1.4 0.9 %add_add_fusion.lists_hbm = s32[16,1024]{1,0:T(8,128)S(1)} fusion(s32[9,1024]{1,0:T(8,128)} %param.9, s32[1,1024]{1,0:T(1,128)} %bitcast.3, s32[16]{0:T(128)S(1)} %pad.2.clone), kind=kLoop, calls=%fused_computation | loop fusion | flops 32768 | bytes 106560 | tf_op jit(solution)/shard_map/concatenate | solution.py:503
  2.3 0.0 copy-start
  2.3 1.4 %copy-done = f32[3,16,64,128]{3,2,1,0:T(8,128)S(1)} copy-done((f32[3,16,64,128]{3,2,1,0:T(8,128)S(1)}, f32[3,16,64,128]{3,2,1,0:T(8,128)}, u32[]{:S(2)}) %copy-start) | copy-done | bytes 1572888
  3.7 0.0 copy-start.1
  3.7 1.0 %copy-done.1 = s32[16,64,128]{2,1,0:T(8,128)S(1)} copy-done((s32[16,64,128]{2,1,0:T(8,128)S(1)}, s32[16,64,128]{2,1,0:T(8,128)}, u32[]{:S(2)}) %copy-start.1) | copy-done | bytes 524312
  4.7 60.8 %shard_map.68 = (f32[3,16,64,128]{3,2,1,0:T(8,128)S(1)}, f32[16,64,128]{2,1,0:T(8,128)S(1)}) custom-call(f32[3,16,64,128]{3,2,1,0:T(8,128)S(1)} %copy-done, s32[16,64,128]{2,1,0:T(8,128)S(1)} %copy-done.1, s32[16,1024]{1,0:T(8,128)S(1)} %add_add_fusion.lists_hbm), custom_call_target="tpu_custom_call" | custom-call | tf_op jit(solution)/shard_map/pallas_call | solution.py:514
  65.5 1.1 %copy.10 = f32[3,16,64,128]{3,2,1,0:T(8,128)} copy(f32[3,16,64,128]{3,2,1,0:T(8,128)S(1)} %get-tuple-element.4) | data formatting | bytes 3145728
  66.7 0.8 %copy.11 = f32[16,64,128]{2,1,0:T(8,128)} copy(f32[16,64,128]{2,1,0:T(8,128)S(1)} %get-tuple-element.5) | data formatting | bytes 1048576
  (1 shorter events, 0.0 us)
Async XLA Ops:
  2.3 1.4 %copy-start = (f32[3,16,64,128]{3,2,1,0:T(8,128)S(1)}, f32[3,16,64,128]{3,2,1,0:T(8,128)}, u32[]{:S(2)}) copy-start(f32[3,16,64,128]{3,2,1,0:T(8,128)} %vel_hbm.1) | copy-start | bytes 4718596
  3.7 1.0 %copy-start.1 = (s32[16,64,128]{2,1,0:T(8,128)S(1)}, s32[16,64,128]{2,1,0:T(8,128)}, u32[]{:S(2)}) copy-start(s32[16,64,128]{2,1,0:T(8,128)} %vf_hbm.1) | copy-start | bytes 1572868
